TPU v7x, 32 devices: a whole 2x2x4 slice. The times are simulated.
32 devices in a mesh: dp: 16 (over z, y, core), blk: 2 (over x).
Axes of the slice: x: 2, y: 2, z: 4, core: 2. Of those that a mesh axis runs over, the one named last changes fastest.
Arguments:
- queries: bfloat16 [16, 125, 256], P('dp'), may hold values from -6 to 6
- memory: bfloat16 [16, 16384, 256], P('dp', 'blk'), may hold values from -6 to 6
- quarter_turns: int32 [16], P('dp'), may hold values from 0 to 3
- token_order: int32 [16, 16384], P('dp', 'blk'), may hold values from 0 to 16383, each once within a row
- lengths: int32 [16], P('dp'), may hold values from 4096 to 16384, as said below
- attn_in: bfloat16 [2, 3, 256, 256], replicated, may hold values from -0.375 to 0.375
- attn_out: bfloat16 [2, 256, 256], replicated, may hold values from -1 to 1
- attn_bias: bfloat16 [2, 3, 256], replicated, may hold values from -3 to 3
- ffn_in: bfloat16 [256, 2048], replicated, may hold values from -0.375 to 0.375
- ffn_in_bias: bfloat16 [2048], replicated, may hold values from -3 to 3
- ffn_out: bfloat16 [2048, 256], replicated, may hold values from -0.125 to 0.125
- ffn_out_bias: bfloat16 [256], replicated, may hold values from -3 to 3
- norm_gain: bfloat16 [3, 256], replicated, may hold values from 0.25 to 1.75
- norm_bias: bfloat16 [3, 256], replicated, may hold values from -2 to 2
- query_pos: bfloat16 [125, 256], replicated, may hold values from -6 to 6
- out_grad: bfloat16 [16, 125, 256], P('dp'), may hold values from -6 to 6
Outputs:
- result: bfloat16 [16, 125, 256], P('dp')
- queries_grad: bfloat16 [16, 125, 256], P('dp')
- memory_grad: bfloat16 [16, 16384, 256], P('dp', 'blk')
- attn_in_grad: float32 [2, 3, 256, 256], replicated
- attn_out_grad: float32 [2, 256, 256], replicated
- attn_bias_grad: float32 [2, 3, 256], replicated
- ffn_in_grad: float32 [256, 2048], replicated
- ffn_in_bias_grad: float32 [2048], replicated
- ffn_out_grad: float32 [2048, 256], replicated
- ffn_out_bias_grad: float32 [256], replicated
- norm_gain_grad: float32 [3, 256], replicated
- norm_bias_grad: float32 [3, 256], replicated
- query_pos_grad: float32 [125, 256], replicated
Inputs may be any that keep to these rules, and one draw needn't show every extreme that they name: `token_order`: each page's row holds every location 0 to 16383 once. `lengths`: a page's valid locations are those below its length; some page has all 16384.
All inputs are finite; a program needn't handle non-finite values.
Results may differ from a plain program's by a relative error of at most 0.0173.
The roundings to bfloat16 on the way count: a program that leaves them out, or rounds other values in their place, can miss the bound.
Values may be sent and summed in bfloat16 or wider, within the bound.
A program may use at most 320 MiB of HBM per device.

v0:
```python
import functools
import math

import jax
import jax.numpy as jnp
import numpy as np
from jax import lax
from jax.experimental import pallas as pl
from jax.experimental.pallas import tpu as pltpu
from jax.sharding import PartitionSpec as P

D = 256
HEADS = 8
HD = D // HEADS
SIDE = 128
NQ = 125
NP = 128
HQ = HEADS * NP
PAIR = 2 * NP
FF = 2048
CHUNK = 1024

masked_score = -1e30
norm_eps = 1e-05
scale = 1.0 / math.sqrt(HD)
log2e = math.log2(math.e)

bf16 = jnp.bfloat16
f32 = jnp.float32

ROWS_F = FF
ROW_POS = 2 * D
ROW_SMALL = 2 * D + NP
ROWS_T = 3 * D
ROWS_K = 3 * D
TILE = 16


def axes_of(pages):
    axes = {"core": (2, 1), "y": (2, 2)}
    stride = 4
    while stride < pages:
        radix = 4 if pages // stride % 4 == 0 else 2
        axes["z%d" % (len(axes) - 2)] = (radix, stride)
        stride *= radix
    axes["x"] = (2, 0)
    return axes


def far_axes(pages):
    return [(name,) for name in axes_of(pages) if name.startswith("z")]


def sum_groups(pages):
    far = far_axes(pages)
    return [("core",), ("y",), *far], [("core", "y"), *far], [("core",), ("x",), ("y",), *far]


def padded(rows, pages):
    unit = TILE * pages
    return (rows + unit - 1) // unit * unit


def position_table():
    half = D // 2
    channel = np.arange(half)
    inverse = np.exp((channel // 2).astype(np.float32) * np.float32(-2.0 * math.log(10000.0) / half))
    angle = (np.arange(SIDE, dtype=np.float32) + 1.0) * np.float32(2.0 * math.pi / SIDE)
    angle = angle[:, None] * inverse
    return np.where(channel % 2 == 0, np.sin(angle), np.cos(angle)).astype(np.float32)


def dot(a, b):
    return jnp.dot(a, b, preferred_element_type=f32)


def dot_nt(a, b):
    return lax.dot_general(a, b, (((1,), (1,)), ((), ())), preferred_element_type=f32)


def dot_tn(a, b):
    return lax.dot_general(a, b, (((0,), (0,)), ((), ())), preferred_element_type=f32)


def row_total(values):
    return jnp.sum(values.astype(f32), axis=0, keepdims=True)


def norm_forward(values):
    average = jnp.mean(values, axis=-1, keepdims=True)
    centred = values - average
    variance = jnp.mean(centred * centred, axis=-1, keepdims=True)
    rstd = lax.rsqrt(variance + norm_eps)
    return centred * rstd, rstd


def norm_backward(grad, normed, rstd, gain):
    grad_normed = grad * gain
    first = jnp.mean(grad_normed, axis=-1, keepdims=True)
    second = jnp.mean(grad_normed * normed, axis=-1, keepdims=True)
    grad_in = rstd * (grad_normed - first - normed * second)
    return grad_in, row_total(grad * normed), row_total(grad)


def spread_rows(rows):
    head = lax.broadcasted_iota(jnp.int32, (NP, D), 1) // HD
    return jnp.concatenate(
        [jnp.where(head == h, rows, 0.0) for h in range(HEADS)], axis=0
    ).astype(bf16)


def spread_cols(cols):
    head = lax.broadcasted_iota(jnp.int32, (D, NP), 0) // HD
    return jnp.concatenate(
        [jnp.where(head == h, cols, 0.0) for h in range(HEADS)], axis=1
    ).astype(bf16)


def project_heads(weight_t, sums):
    high = sums.astype(bf16)
    low = (sums - high.astype(f32)).astype(bf16)
    return own_blocks(
        [
            dot(weight_t[pair_rows(p)], high[:, pair_cols(p)])
            + dot(weight_t[pair_rows(p)], low[:, pair_cols(p)])
            for p in range(4)
        ]
    )


def own_blocks(pairs):
    parts = []
    for pair in pairs:
        parts += [pair[:HD, :NP], pair[HD:, NP:]]
    return jnp.concatenate(parts, axis=0)


def head_rows(row):
    return jnp.concatenate([row[:, NP * h : NP * h + NP] for h in range(HEADS)], axis=0)


def head_line(rows):
    return jnp.concatenate([rows[h : h + 1] for h in range(HEADS)], axis=1)


def per_channel(rows):
    return jnp.concatenate(
        [jnp.broadcast_to(rows[h : h + 1], (HD, NP)) for h in range(HEADS)], axis=0
    )


def head_sums(cols):
    return jnp.concatenate(
        [jnp.sum(cols[HD * h : HD * h + HD], axis=0, keepdims=True) for h in range(HEADS)], axis=0
    )


def pair_cols(p):
    return slice(PAIR * p, PAIR * p + PAIR)


def pair_rows(p):
    return slice(2 * HD * p, 2 * HD * p + 2 * HD)


class Place:
    def __init__(self, pages):
        self.axes = axes_of(pages)
        self.page = lax.axis_index("dp")
        self.member = lax.axis_index("blk")
        self.digit = {
            name: self.member if name == "x" else lax.rem(self.page // stride, radix)
            for name, (radix, stride) in self.axes.items()
        }

    def size(self, group):
        return math.prod(self.axes[name][0] for name in group)

    def index(self, group):
        index = 0
        for name in group:
            index = index * self.axes[name][0] + self.digit[name]
        return index

    def peer(self, group, hop):
        index = lax.rem(self.index(group) + hop, self.size(group))
        page, member, rest = self.page, self.member, index
        for name in reversed(group):
            radix, stride = self.axes[name]
            digit = lax.rem(rest, radix)
            rest = rest // radix
            if name == "x":
                member = digit
            else:
                page = page + (digit - self.digit[name]) * stride
        return (page, member), index


class PageSum:
    def __init__(self, place, groups, back, rows, landing, whole, sent, arrived):
        self.place, self.groups, self.back = place, groups, back
        self.rows, self.landing, self.whole = rows, landing, whole
        self.sent, self.arrived = sent, arrived
        self.slots = 0
        self.extents = [rows.shape[0]]
        self.bases = [0]
        self.landings = []
        at = 0
        for group in groups:
            size = place.size(group)
            extent = self.extents[-1] // size
            self.landings.append(at)
            at += (size - 1) * extent
            self.bases.append(pl.multiple_of(self.bases[-1] + place.index(group) * extent, TILE))
            self.extents.append(extent)
        last = len(groups)
        moves = [self.scatter_moves(s) for s in range(last)]
        near = {"all": 0, "across": 1, "sides": 2}[back]
        moves += [self.gather_moves(s) for s in range(last - 1, near - 1, -1)]
        if back == "sides":
            moves += [self.side_moves(), self.corner_moves(), self.core_moves()]
        elif back == "across":
            moves += [self.across_moves(), self.core_moves()]
        self.phases = [functools.partial(self.step, moves, k) for k in range(len(moves) + 1)]

    @staticmethod
    def landing_rows(pages, groups, rows):
        axes = axes_of(pages)
        total, extent = 0, rows
        for group in groups:
            size = math.prod(axes[name][0] for name in group)
            extent //= size
            total += (size - 1) * extent
        return total

    def step(self, moves, k):
        last = len(self.groups)
        if k > 0:
            for move in moves[k - 1]:
                self.copy(*move).wait()
        if 0 < k <= last:
            total = self.scatter_sum(k - 1)
            region = pl.ds(self.bases[k], self.extents[k])
            if k < last:
                self.rows[region] = total
            elif len(self.whole.shape) == 3:
                self.whole[self.place.member, region] = total
            else:
                self.whole[region] = total
        if k < len(moves):
            for move in moves[k]:
                self.copy(*move).start()

    def copy(self, slot, source, target, device):
        return pltpu.make_async_remote_copy(
            src_ref=source(),
            dst_ref=target(),
            send_sem=self.sent.at[slot],
            recv_sem=self.arrived.at[slot],
            device_id=device,
            device_id_type=pl.DeviceIdType.MESH,
        )

    def new_slot(self):
        self.slots += 1
        return self.slots - 1

    def same(self, device, view):
        return (self.new_slot(), view, view, device)

    def scatter_moves(self, step):
        group = self.groups[step]
        extent = self.extents[step + 1]
        moves = []
        for hop in range(1, self.place.size(group)):
            device, other = self.place.peer(group, hop)
            start = pl.multiple_of(self.bases[step] + other * extent, TILE)
            landing = self.landings[step] + (hop - 1) * extent
            moves.append(
                (
                    self.new_slot(),
                    functools.partial(self.part, self.rows, start, extent),
                    functools.partial(self.part, self.landing, landing, extent),
                    device,
                )
            )
        return moves

    @staticmethod
    def part(ref, start, extent):
        return ref.at[pl.ds(start, extent)]

    def half(self, member, start, extent):
        if len(self.whole.shape) == 3:
            return self.whole.at[member, pl.ds(start, extent)]
        return self.whole.at[pl.ds(start, extent)]

    def scatter_sum(self, step):
        extent = self.extents[step + 1]
        total = self.rows[pl.ds(self.bases[step + 1], extent)].astype(f32)
        for hop in range(1, self.place.size(self.groups[step])):
            landing = self.landings[step] + (hop - 1) * extent
            total = total + self.landing[pl.ds(landing, extent)].astype(f32)
        return total.astype(bf16)

    def gather_moves(self, step):
        group = self.groups[step]
        view = functools.partial(self.half, self.place.member, self.bases[step + 1], self.extents[step + 1])
        return [
            self.same(self.place.peer(group, hop)[0], view) for hop in range(1, self.place.size(group))
        ]

    def own_quarter(self):
        step = 2 if len(self.groups[0]) == 1 else 1
        return self.bases[step], self.extents[step]

    def side_moves(self):
        view = functools.partial(self.half, self.place.member, *self.own_quarter())
        return [self.same(self.place.peer((name,), 1)[0], view) for name in ("y", "x")]

    def corner_moves(self):
        base, extent = self.own_quarter()
        other = pl.multiple_of(base + (1 - 2 * self.place.digit["y"]) * extent, TILE)
        view = functools.partial(self.half, self.place.member, other, extent)
        return [self.same(self.place.peer(("x",), 1)[0], view)]

    def across_moves(self):
        view = functools.partial(self.half, self.place.member, *self.own_quarter())
        return [self.same(self.place.peer(("x", "y"), hop)[0], view) for hop in range(1, 4)]

    def core_moves(self):
        extent = self.extents[0] // 2
        start = pl.multiple_of(self.place.digit["core"] * extent, TILE)
        device, _ = self.place.peer(("core",), 1)
        return [self.same(device, functools.partial(self.half, m, start, extent)) for m in range(2)]


def clear_rest(ref, used):
    if ref.shape[0] > used:
        ref[used:] = jnp.zeros((ref.shape[0] - used, D), ref.dtype)


def layer_kernel(
    tokens,
    pages,
    queries_in,
    memory_hbm,
    turns_in,
    order_in,
    lengths_in,
    attn_in,
    attn_out,
    attn_bias,
    ffn_in_hbm,
    ffn_in_bias,
    ffn_out_hbm,
    ffn_out_bias,
    norm_gain,
    norm_bias,
    pos_in,
    out_grad_in,
    table_in,
    result_hbm,
    queries_grad_hbm,
    memory_grad_hbm,
    whole_f_hbm,
    whole_t_hbm,
    whole_k_hbm,
    memory_s,
    key_in_s,
    probs_s,
    grad_scores_s,
    code_s,
    query_kt,
    grad_vt,
    back_s,
    table_s,
    top_s,
    highest_s,
    shifts_s,
    factor_s,
    total_s,
    mixed_s,
    pad_s,
    result_out,
    queries_grad_out,
    send_a,
    recv_a,
    send_t,
    recv_t,
    send_b,
    recv_b,
    small_s,
    rows_f,
    landing_f,
    whole_f,
    rows_t,
    landing_t,
    whole_t,
    rows_k,
    landing_k,
    whole_k,
    load_sem,
    store_sem,
    link_sem,
    sent_f,
    arrived_f,
    sent_t,
    arrived_t,
    sent_k,
    arrived_k,
):
    member = lax.axis_index("blk")
    partner = (lax.axis_index("dp"), 1 - member)
    chunks = tokens // CHUNK

    place = Place(pages)
    groups_f, groups_t, groups_k = sum_groups(pages)
    sum_f = PageSum(place, groups_f, "sides", rows_f, landing_f, whole_f, sent_f, arrived_f)
    sum_t = PageSum(place, groups_t, "across", rows_t, landing_t, whole_t, sent_t, arrived_t)
    sum_k = PageSum(place, groups_k, "all", rows_k, landing_k, whole_k, sent_k, arrived_k)

    barrier = pltpu.get_barrier_semaphore()
    peers = [
        place.peer(group, hop)[0]
        for group in [("x", "core", "y"), *far_axes(pages)]
        for hop in range(1, place.size(group))
    ]
    for peer in peers:
        pl.semaphore_signal(barrier, inc=1, device_id=peer, device_id_type=pl.DeviceIdType.MESH)

    load_memory = pltpu.make_async_copy(memory_hbm.at[0], memory_s, load_sem.at[0])
    half = FF // 2
    ffn_in_s = [grad_scores_s.at[D * k : D * k + D] for k in range(2)]
    ffn_out_s = grad_scores_s.at[2 * D : 2 * D + FF, :D]
    free = 2 * D + FF
    active_s = [grad_scores_s.at[free + NP * k : free + NP * k + NP] for k in range(2)]
    slope_s = [grad_scores_s.at[free + NP * k : free + NP * k + NP] for k in range(2, 4)]
    load_ffn = [
        pltpu.make_async_copy(ffn_in_hbm.at[:, half * k : half * k + half], ffn_in_s[k], load_sem.at[1 + k])
        for k in range(2)
    ]
    load_ffn.append(pltpu.make_async_copy(ffn_out_hbm, ffn_out_s, load_sem.at[3]))
    load_memory.start()
    for load in load_ffn:
        load.start()

    pairs = [attn_bias[j].astype(f32) for j in range(3)]
    bias = jnp.concatenate([pair[k : k + 1] for k in range(2) for pair in pairs], axis=0)
    gain = norm_gain[...].astype(f32)
    shift = norm_bias[...].astype(f32)

    order = order_in[...]
    turn = turns_in[0]
    row_at = order >> 7
    col_at = order & 127
    top = SIDE - 1
    row_new = jnp.where(
        turn == 0, row_at, jnp.where(turn == 1, col_at, jnp.where(turn == 2, top - row_at, top - col_at))
    )
    col_new = jnp.where(
        turn == 0, col_at, jnp.where(turn == 1, top - row_at, jnp.where(turn == 2, top - col_at, row_at))
    )
    past = jnp.where(order < lengths_in[0], 0, SIDE * SIDE)
    code_s[...] = (row_new * SIDE + col_new + past).astype(f32)

    pad_s[...] = jnp.zeros_like(pad_s)
    pad_s[0, :NQ] = queries_in[0].astype(f32)
    pad_s[1, :NQ] = pos_in[...].astype(f32)
    pad_s[2, :NQ] = out_grad_in[0].astype(f32)
    queries_f = pad_s[0]
    pos_f = pad_s[1]
    queries_b = queries_f.astype(bf16)
    mixed_q = (queries_f + pos_f).astype(bf16)
    query_self = (dot(mixed_q, attn_in[0, 0]) + bias[0:1]).astype(bf16)
    key_self = dot(mixed_q, attn_in[0, 1]).astype(bf16)
    value_self = (dot(queries_b, attn_in[0, 2]) + bias[1:2]).astype(bf16)
    scores = dot(key_self, spread_cols(query_self.astype(f32).T)) * scale
    own_key = lax.broadcasted_iota(jnp.int32, (NP, HQ), 0) < NQ
    scores = jnp.where(own_key, scores, masked_score)
    raised = jnp.exp(scores - jnp.max(scores, axis=0, keepdims=True))
    probs_self = raised / jnp.sum(raised, axis=0, keepdims=True)
    probs_self_b = probs_self.astype(bf16)
    value_t = value_self.astype(f32).T.astype(bf16)
    attended = own_blocks(
        [dot(value_t[pair_rows(p)], probs_self_b[:, pair_cols(p)]) for p in range(4)]
    ).T.astype(bf16)
    first_normed, first_rstd = norm_forward(queries_f + dot(attended, attn_out[0]) + bias[2:3])
    first = first_normed * gain[0:1] + shift[0:1]
    cross_q = (first + pos_f).astype(bf16)
    query_c = (dot(cross_q, attn_in[1, 0]) + bias[3:4]).astype(bf16)
    query_x = spread_rows(query_c.astype(f32))
    query_k = dot(attn_in[1, 1], spread_cols(query_c.astype(f32).T))
    query_kt[...] = (query_k * (scale * log2e)).astype(bf16)
    back_s[:HQ] = (dot_nt(query_x, attn_in[1, 1]) * scale).astype(bf16)
    table = table_in[...]
    nothing = jnp.zeros((SIDE, D // 2), f32)
    table = jnp.concatenate(
        [jnp.concatenate([table, nothing], axis=1), jnp.concatenate([nothing, table], axis=1)], axis=0
    )
    table_high = table.astype(bf16)
    table_s[: 2 * SIDE] = table_high
    table_s[2 * SIDE :] = (table - table_high.astype(f32)).astype(bf16)

    load_memory.wait()
    def mask_view(i):
        side, place = i // (chunks // 2), lax.rem(i, chunks // 2)
        return grad_scores_s.at[
            pl.ds(pl.multiple_of(tokens // 2 + place * CHUNK, CHUNK), CHUNK),
            pl.ds(pl.multiple_of(side * NP, NP), NP),
        ]

    lane = lax.broadcasted_iota(jnp.int32, (CHUNK, NP), 1)

    @pl.loop(0, chunks)
    def _(i):
        rows = pl.ds(pl.multiple_of(i * CHUNK, CHUNK), CHUNK)
        line = code_s[:, rows]
        code = jnp.concatenate(
            [
                jnp.broadcast_to(line[:, NP * j : NP * j + NP], (NP, NP)).T
                for j in range(CHUNK // NP)
            ],
            axis=0,
        ).astype(jnp.int32)
        row_hot = jnp.where(((code >> 7) & 127) == lane, 1.0, 0.0).astype(bf16)
        col_hot = jnp.where((code & 127) == lane, 1.0, 0.0).astype(bf16)
        hot = jnp.concatenate([row_hot, col_hot, row_hot, col_hot], axis=1)
        masked = jnp.where(code < SIDE * SIDE, 0.0, masked_score)
        mask_view(i)[...] = masked.astype(bf16)
        key_in_s[rows] = (memory_s[rows].astype(f32) + dot(hot, table_s[...])).astype(bf16)

    def score_pair(p, key_in, mask, score_s):
        cols = pair_cols(p)
        part = dot(key_in, query_kt[:, cols]) + mask
        score_s[:, cols] = part
        top_s[:, cols] = jnp.max(part.reshape(CHUNK // 8, 8, PAIR), axis=0)

    def score_operands(i):
        rows = pl.ds(pl.multiple_of(i * CHUNK, CHUNK), CHUNK)
        mask = mask_view(i)[...].astype(f32)
        return key_in_s[rows], jnp.concatenate([mask, mask], axis=1)

    def attend_all(score_s):
        operands = score_operands(0)
        for p in range(4):
            score_pair(p, *operands, score_s)

        @pl.loop(0, chunks)
        def _(i):
            rows = pl.ds(pl.multiple_of(i * CHUNK, CHUNK), CHUNK)
            memory_ct = memory_s[rows].T
            operands = score_operands(jnp.minimum(i + 1, chunks - 1))
            for p in range(4):
                cols = pair_cols(p)
                before = highest_s[0:1, cols]
                highest = jnp.maximum(before, jnp.max(top_s[:, cols], axis=0, keepdims=True))
                highest_s[0:1, cols] = highest
                shifts_s[pl.ds(i, 1), cols] = highest
                fade = jnp.exp2(before - highest)
                raised = jnp.exp2(score_s[:, cols] - highest)
                sums = jnp.sum(raised.reshape(CHUNK // 8, 8, PAIR), axis=0)
                total_s[:, cols] = total_s[:, cols] * fade + sums
                probs_s[rows, cols] = raised.astype(bf16)
                mixed_s[:, cols] = mixed_s[:, cols] * fade + dot(memory_ct, probs_s[rows, cols])
                score_pair(p, *operands, score_s)

    highest_s[0:1] = jnp.full((1, HQ), -3e38, f32)
    total_s[...] = jnp.zeros_like(total_s)
    mixed_s[...] = jnp.zeros_like(mixed_s)
    pl.run_scoped(attend_all, pltpu.VMEM((CHUNK, HQ), f32))
    highest_own = highest_s[0:1]
    total_own = jnp.sum(total_s[...], axis=0, keepdims=True)

    value_wt = attn_in[1, 2].astype(f32).T.astype(bf16)
    key_wt = attn_in[1, 1].astype(f32).T.astype(bf16)
    send_a[...] = project_heads(value_wt, mixed_s[...]).astype(bf16)
    send_t[:HEADS] = head_rows(highest_own)
    send_t[HEADS:] = head_rows(total_own)
    pl.semaphore_wait(barrier, len(peers))
    swap_a = pltpu.make_async_remote_copy(
        src_ref=send_a,
        dst_ref=recv_a,
        send_sem=link_sem.at[0],
        recv_sem=link_sem.at[1],
        device_id=partner,
        device_id_type=pl.DeviceIdType.MESH,
    )
    swap_t = pltpu.make_async_remote_copy(
        src_ref=send_t,
        dst_ref=recv_t,
        send_sem=link_sem.at[4],
        recv_sem=link_sem.at[5],
        device_id=partner,
        device_id_type=pl.DeviceIdType.MESH,
    )
    swap_a.start()
    swap_t.start()
    swap_a.wait()
    swap_t.wait()
    is_first = member == 0
    own, other = send_a[...].astype(f32), recv_a[...].astype(f32)
    left = jnp.where(is_first, own, other)
    right = jnp.where(is_first, other, own)
    own, other = send_t[...], recv_t[...]
    left_t = jnp.where(is_first, own, other)
    right_t = jnp.where(is_first, other, own)
    highest = jnp.maximum(left_t[:HEADS], right_t[:HEADS])
    fade_l = jnp.exp2(left_t[:HEADS] - highest)
    fade_r = jnp.exp2(right_t[:HEADS] - highest)
    total = left_t[HEADS:] * fade_l + right_t[HEADS:] * fade_r
    mixed_t = left * per_channel(fade_l / total) + right * per_channel(fade_r / total)
    log_total = head_line(highest + jnp.log2(total))
    own_share = jnp.exp2(highest_own - log_total)
    factor_s[...] = jnp.exp2(shifts_s[...] - log_total)
    attended_c = (mixed_t.T + bias[4:5]).astype(bf16)

    second_normed, second_rstd = norm_forward(first + dot(attended_c, attn_out[1]) + bias[5:6])
    second = second_normed * gain[1:2] + shift[1:2]
    ffn_input = second.astype(bf16)
    load_ffn[0].wait()
    load_ffn[1].wait()
    blocks = [(j // 4, slice(D * j, D * j + D), slice(j % 4 * D, j % 4 * D + D)) for j in range(FF // D)]
    hidden_bias = ffn_in_bias[...].astype(f32).reshape(1, FF)
    def feed_forward(gate_s):
        for k, cols, part in blocks:
            hidden = dot(ffn_input, ffn_in_s[k][:, part]) + hidden_bias[:, cols]
            half_gate = 0.5 + 0.5 * lax.erf(hidden * math.sqrt(0.5))
            active_s[k][:, part] = (hidden * half_gate).astype(bf16)
            gate_s[:, cols] = half_gate + hidden * jnp.exp(hidden * hidden * -0.5) * (
                1.0 / math.sqrt(2.0 * math.pi)
            )
        load_ffn[2].wait()
        third_normed, third_rstd = norm_forward(
            second
            + dot(active_s[0][...], ffn_out_s[:half])
            + dot(active_s[1][...], ffn_out_s[half:])
            + ffn_out_bias[...].astype(f32).reshape(1, D)
        )
        result_out[...] = (third_normed * gain[2:3] + shift[2:3])[:NQ].astype(bf16)
        grad_third, gain_grad_2, shift_grad_2 = norm_backward(
            pad_s[2], third_normed, third_rstd, gain[2:3]
        )
        grad_branch_f = grad_third.astype(bf16)
        for k, cols, part in blocks:
            grad_hidden = dot_nt(grad_branch_f, ffn_out_s[cols]) * gate_s[:, cols]
            slope_s[k][:, part] = grad_hidden.astype(bf16)
        return grad_third, gain_grad_2, shift_grad_2, grad_branch_f

    grad_third, gain_grad_2, shift_grad_2, grad_branch_f = pl.run_scoped(
        feed_forward, pltpu.VMEM((NP, FF), f32)
    )
    grad_second = grad_third + dot_nt(slope_s[0][...], ffn_in_s[0][...])
    grad_second += dot_nt(slope_s[1][...], ffn_in_s[1][...])
    grad_second_in, gain_grad_1, shift_grad_1 = norm_backward(
        grad_second, second_normed, second_rstd, gain[1:2]
    )
    grad_branch_c = grad_second_in.astype(bf16)
    ffn_input_t = second.T.astype(bf16)

    @pl.when(member == 0)
    def _():
        for k, cols, part in blocks:
            rows_f[cols] = dot(ffn_input_t, slope_s[k][:, part]).astype(bf16)

    @pl.when(member == 1)
    def _():
        for k, cols, part in blocks:
            rows_f[cols] = dot_tn(active_s[k][:, part], grad_branch_f).astype(bf16)

    is_first = member == 0
    out_grad_c = dot_tn(attended_c, grad_branch_c)
    rows_k[2 * D : 3 * D] = jnp.where(is_first, out_grad_c, 0.0).astype(bf16)

    clear_rest(rows_f, ROWS_F)
    clear_rest(rows_t, ROWS_T)
    clear_rest(rows_k, ROWS_K)
    sum_f.phases[0]()
    grad_attended_c = dot_nt(grad_branch_c, attn_out[1]).astype(bf16).astype(f32)
    small_s[:16] = jnp.concatenate(
        [row_total(slope_s[k][:, part]) for k, _, part in blocks]
        + [
            row_total(grad_branch_f),
            row_total(grad_branch_c),
            gain_grad_2,
            shift_grad_2,
            gain_grad_1,
            shift_grad_1,
            row_total(grad_attended_c),
            jnp.zeros((1, D), f32),
        ],
        axis=0,
    )

    store_result = pltpu.make_async_copy(result_out, result_hbm, load_sem.at[7])
    store_result.start()

    grad_attended_t = grad_attended_c.T
    grad_x = spread_rows(grad_attended_c)
    grad_v = dot(attn_in[1, 2], spread_cols(grad_attended_t))
    grad_vt[...] = grad_v.astype(bf16)
    back_s[HQ:] = grad_v.T.astype(bf16)
    inner = head_line(head_sums(grad_attended_t * mixed_t))
    rows_k[D : 2 * D] = dot((mixed_s[...] * own_share).astype(bf16), grad_x).astype(bf16)
    mixed_s[...] = jnp.zeros_like(mixed_s)

    queue_f = sum_f.phases[1:]
    queue_t = list(sum_t.phases)
    queue_k = list(sum_k.phases)

    def take(queue):
        if queue:
            queue.pop(0)()

    def at(i, steps):
        for step, queue in steps:
            pl.when(i == (step * chunks) // 16)(queue.pop(0))

    @pl.loop(0, chunks)
    def _(i):
        rows = pl.ds(pl.multiple_of(i * CHUNK, CHUNK), CHUNK)
        key_ct = key_in_s[rows].T
        memory_c = memory_s[rows]
        for p in range(4):
            cols = pair_cols(p)
            grad_probs = dot(memory_c, grad_vt[:, cols])
            probs = probs_s[rows, cols].astype(f32) * factor_s[pl.ds(i, 1), cols]
            probs_s[rows, cols] = probs.astype(bf16)
            grad_scores_s[rows, cols] = (probs * (grad_probs - inner[:, cols])).astype(bf16)
        mixed_s[...] += dot(key_ct, grad_scores_s[rows])
        at(i, [(3, queue_f), (9, queue_f), (15, queue_f)])

    send_b[...] = (project_heads(key_wt, mixed_s[...]) * scale).astype(bf16)
    swap_b = pltpu.make_async_remote_copy(
        src_ref=send_b,
        dst_ref=recv_b,
        send_sem=link_sem.at[2],
        recv_sem=link_sem.at[3],
        device_id=partner,
        device_id_type=pl.DeviceIdType.MESH,
    )
    swap_b.start()
    query_x = spread_rows(query_c.astype(f32))
    rows_k[:D] = (dot(mixed_s[...].astype(bf16), query_x) * scale).astype(bf16)
    take(queue_k)
    swap_b.wait()
    take(queue_f)
    take(queue_k)
    grad_query_c = (send_b[...].astype(f32) + recv_b[...].astype(f32)).T.astype(bf16)

    cross_pos_grad = dot_nt(grad_query_c, attn_in[1, 0])
    grad_first_in, gain_grad_0, shift_grad_0 = norm_backward(
        grad_second_in + cross_pos_grad, first_normed, first_rstd, gain[0:1]
    )
    grad_branch = grad_first_in.astype(bf16)
    grad_attended = dot_nt(grad_branch, attn_out[0]).astype(bf16).astype(f32)
    take(queue_k)
    grad_probs = dot(value_self, spread_cols(grad_attended.T))
    inner_self = jnp.sum(probs_self * grad_probs, axis=0, keepdims=True)
    grad_scores = (probs_self * (grad_probs - inner_self)).astype(bf16)
    key_t = key_self.astype(f32).T.astype(bf16)
    grad_query_s = (
        own_blocks([dot(key_t[pair_rows(p)], grad_scores[:, pair_cols(p)]) for p in range(4)]) * scale
    ).T.astype(bf16)
    grad_key_s = (dot(grad_scores, spread_rows(query_self.astype(f32))) * scale).astype(bf16)
    grad_value_s = dot(probs_self_b, spread_rows(grad_attended)).astype(bf16)
    grad_mixed_q = dot_nt(grad_query_s, attn_in[0, 0]) + dot_nt(grad_key_s, attn_in[0, 1])
    queries_grad_out[...] = (grad_first_in + grad_mixed_q + dot_nt(grad_value_s, attn_in[0, 2]))[
        :NQ
    ].astype(bf16)
    store_queries = pltpu.make_async_copy(queries_grad_out, queries_grad_hbm, load_sem.at[8])
    store_queries.start()
    small_s[16:] = jnp.concatenate(
        [
            row_total(grad_query_s),
            row_total(grad_value_s),
            row_total(grad_branch),
            row_total(grad_query_c),
            gain_grad_0,
            shift_grad_0,
            jnp.zeros((10, D), f32),
        ],
        axis=0,
    )
    @pl.when(member == 0)
    def _():
        rows_t[:D] = dot_tn(mixed_q, grad_query_s).astype(bf16)
        rows_t[D : 2 * D] = dot_tn(mixed_q, grad_key_s).astype(bf16)
        rows_t[2 * D : 3 * D] = dot_tn(queries_b, grad_value_s).astype(bf16)

    @pl.when(member == 1)
    def _():
        rows_t[:D] = dot_tn(cross_q, grad_query_c).astype(bf16)
        rows_t[D : 2 * D] = dot_tn(attended, grad_branch).astype(bf16)
        rows_t[ROW_POS:ROW_SMALL] = (grad_mixed_q + cross_pos_grad).astype(bf16)
        rows_t[ROW_SMALL : ROW_SMALL + 32] = small_s[...].astype(bf16)
        rows_t[ROW_SMALL + 32 : ROWS_T] = jnp.zeros((ROWS_T - ROW_SMALL - 32, D), bf16)

    take(queue_t)
    take(queue_k)
    take(queue_f)

    @pl.loop(0, chunks)
    def _(i):
        rows = pl.ds(pl.multiple_of(i * CHUNK, CHUNK), CHUNK)
        both = jnp.concatenate([grad_scores_s[rows], probs_s[rows]], axis=1)
        memory_s[rows] = dot(both, back_s[...]).astype(bf16)
        pltpu.make_async_copy(memory_s.at[rows], memory_grad_hbm.at[0, rows], store_sem.at[i]).start()
        at(
            i,
            [
                (3, queue_t),
                (4, queue_k),
                (7, queue_t),
                (8, queue_k),
                (9, queue_f),
                (11, queue_t),
                (12, queue_k),
                (15, queue_t),
            ],
        )

    while queue_f:
        take(queue_f)
    stores = [
        pltpu.make_async_copy(whole, target, load_sem.at[4 + k])
        for k, (whole, target) in enumerate(
            (
                (whole_f, whole_f_hbm),
                (whole_t, whole_t_hbm),
                (whole_k, whole_k_hbm),
            )
        )
    ]
    stores[0].start()
    while queue_t or queue_k:
        take(queue_t)
        take(queue_k)
    for store in stores[1:]:
        store.start()

    @pl.loop(0, chunks)
    def _(i):
        rows = pl.ds(pl.multiple_of(i * CHUNK, CHUNK), CHUNK)
        pltpu.make_async_copy(memory_s.at[rows], memory_grad_hbm.at[0, rows], store_sem.at[i]).wait()

    for store in [*stores, store_result, store_queries]:
        store.wait()


def finish_kernel(
    result_in,
    queries_grad_in,
    memory_grad_in,
    whole_f_hbm,
    whole_t_hbm,
    whole_k_hbm,
    result_hbm,
    queries_grad_hbm,
    memory_grad,
    attn_in_hbm,
    attn_out_hbm,
    attn_bias_hbm,
    ffn_in_hbm,
    ffn_in_bias_hbm,
    ffn_out_hbm,
    ffn_out_bias_hbm,
    norm_gain_hbm,
    norm_bias_hbm,
    query_pos_hbm,
    moved,
    whole_f,
    whole_t,
    whole_k,
    result,
    queries_grad,
    attn_in_grad,
    attn_out_grad,
    attn_bias_grad,
    ffn_in_grad,
    ffn_in_bias_grad,
    ffn_out_grad,
    ffn_out_bias_grad,
    norm_gain_grad,
    norm_bias_grad,
    query_pos_grad,
    in_sem,
    out_sem,
    sum_sem,
    grad_sem,
):
    pieces = in_sem.shape[0]
    piece = moved.shape[0] // pieces

    def fetch(j):
        rows = pl.ds(piece * j, piece)
        return pltpu.make_async_copy(memory_grad_in.at[0, rows], moved.at[rows], in_sem.at[j])

    def write(j):
        rows = pl.ds(piece * j, piece)
        return pltpu.make_async_copy(moved.at[rows], memory_grad.at[0, rows], out_sem.at[j])

    sums = [
        (whole_t_hbm, whole_t),
        (whole_k_hbm, whole_k),
        (whole_f_hbm, whole_f),
        (result_in, result),
        (queries_grad_in, queries_grad),
    ]
    loads = [pltpu.make_async_copy(*pair, sum_sem.at[j]) for j, pair in enumerate(sums)]
    for load in loads:
        load.start()
    for j in range(pieces):
        fetch(j).start()
    blocks = FF // D
    stores = []

    def store(source, target):
        stores.append(pltpu.make_async_copy(source, target, grad_sem.at[len(stores)]))
        stores[-1].start()

    loads[0].wait()
    loads[1].wait()
    for j in range(3):
        attn_in_grad[0, j] = whole_t[0, D * j : D * j + D].astype(f32)
    attn_in_grad[1, 0] = whole_t[1, :D].astype(f32)
    attn_in_grad[1, 1] = whole_k[:D].astype(f32)
    attn_in_grad[1, 2] = whole_k[D : 2 * D].astype(f32)
    store(attn_in_grad, attn_in_hbm)
    attn_out_grad[0] = whole_t[1, D : 2 * D].astype(f32)
    attn_out_grad[1] = whole_k[2 * D : 3 * D].astype(f32)
    store(attn_out_grad, attn_out_hbm)
    loads[2].wait()
    for k in range(2):
        half = slice(FF // 2 * k, FF // 2 * (k + 1))
        ffn_out_grad[half] = whole_f[1, half].astype(f32)
        store(ffn_out_grad.at[half], ffn_out_hbm.at[half])
    for k in range(2):
        half = slice(FF // 2 * k, FF // 2 * (k + 1))
        for j in range(blocks // 2 * k, blocks // 2 * (k + 1)):
            at = slice(D * j, D * j + D)
            ffn_in_grad[:, at] = whole_f[0, at].astype(f32)
        store(ffn_in_grad.at[:, half], ffn_in_hbm.at[:, half])
    for j in range(pieces):
        fetch(j).wait()
        write(j).start()
    loads[3].wait()
    store(result, result_hbm.at[0])
    loads[4].wait()
    store(queries_grad, queries_grad_hbm.at[0])
    query_pos_grad[...] = whole_t[1, ROW_POS:ROW_SMALL].astype(f32)[:NQ]
    store(query_pos_grad, query_pos_hbm)
    small = whole_t[1, ROW_SMALL : ROW_SMALL + 32].astype(f32)
    ffn_in_bias_grad[...] = jnp.concatenate([small[j : j + 1] for j in range(blocks)], axis=1)
    store(ffn_in_bias_grad, ffn_in_bias_hbm)
    ffn_out_bias_grad[...] = small[8:9]
    store(ffn_out_bias_grad, ffn_out_bias_hbm)
    for j, (own, cross) in enumerate(((16, 19), (17, 14), (18, 9))):
        attn_bias_grad[j, 0:1] = small[own : own + 1]
        attn_bias_grad[j, 1:2] = small[cross : cross + 1]
    store(attn_bias_grad, attn_bias_hbm)
    for j, (gain, shift) in enumerate(((20, 21), (12, 13), (10, 11))):
        norm_gain_grad[j : j + 1] = small[gain : gain + 1]
        norm_bias_grad[j : j + 1] = small[shift : shift + 1]
    store(norm_gain_grad, norm_gain_hbm)
    store(norm_bias_grad, norm_bias_hbm)
    for j in range(pieces):
        write(j).wait()
    for copy in stores:
        copy.wait()


def body(
    pages,
    queries,
    memory,
    quarter_turns,
    token_order,
    lengths,
    attn_in,
    attn_out,
    attn_bias,
    ffn_in,
    ffn_in_bias,
    ffn_out,
    ffn_out_bias,
    norm_gain,
    norm_bias,
    query_pos,
    out_grad,
):
    tokens = memory.shape[1]
    chunks = tokens // CHUNK
    groups_f, groups_t, groups_k = sum_groups(pages)
    summed = [
        (padded(ROWS_F, pages), groups_f),
        (padded(ROWS_T, pages), groups_t),
        (padded(ROWS_K, 2 * pages), groups_k),
    ]
    whole_shapes = [(2, rows, D) for rows, _ in summed[:2]] + [(summed[2][0], D)]
    sum_buffers = []
    for (rows, groups), shape in zip(summed, whole_shapes):
        landing = PageSum.landing_rows(pages, groups, rows)
        sum_buffers += [pltpu.VMEM(each, bf16) for each in ((rows, D), (landing, D), shape)]
    copies = 32
    vmem = pl.BlockSpec(memory_space=pltpu.VMEM)
    smem = pl.BlockSpec(memory_space=pltpu.SMEM)
    anywhere = pl.BlockSpec(memory_space=pl.ANY)
    parts = pl.pallas_call(
        functools.partial(layer_kernel, tokens, pages),
        out_shape=[
            jax.ShapeDtypeStruct((NQ, D), bf16),
            jax.ShapeDtypeStruct((NQ, D), bf16),
            jax.ShapeDtypeStruct((1, tokens, D), bf16),
            *(jax.ShapeDtypeStruct(shape, bf16) for shape in whole_shapes),
        ],
        in_specs=[
            vmem,
            anywhere,
            smem,
            vmem,
            smem,
            vmem,
            vmem,
            vmem,
            anywhere,
            vmem,
            anywhere,
            vmem,
            vmem,
            vmem,
            vmem,
            vmem,
            vmem,
        ],
        out_specs=[anywhere] * 6,
        scratch_shapes=[
            pltpu.VMEM((tokens, D), bf16),
            pltpu.VMEM((tokens, D), bf16),
            pltpu.VMEM((tokens, HQ), bf16),
            pltpu.VMEM((tokens, HQ), bf16),
            pltpu.VMEM((1, tokens), f32),
            pltpu.VMEM((D, HQ), bf16),
            pltpu.VMEM((D, HQ), bf16),
            pltpu.VMEM((2 * HQ, D), bf16),
            pltpu.VMEM((4 * SIDE, D), bf16),
            pltpu.VMEM((8, HQ), f32),
            pltpu.VMEM((8, HQ), f32),
            pltpu.VMEM((chunks, HQ), f32),
            pltpu.VMEM((chunks, HQ), f32),
            pltpu.VMEM((8, HQ), f32),
            pltpu.VMEM((D, HQ), f32),
            pltpu.VMEM((3, NP, D), f32),
            pltpu.VMEM((NQ, D), bf16),
            pltpu.VMEM((NQ, D), bf16),
            pltpu.VMEM((D, NP), bf16),
            pltpu.VMEM((D, NP), bf16),
            pltpu.VMEM((2 * HEADS, NP), f32),
            pltpu.VMEM((2 * HEADS, NP), f32),
            pltpu.VMEM((D, NP), bf16),
            pltpu.VMEM((D, NP), bf16),
            pltpu.VMEM((32, D), f32),
            *sum_buffers,
            pltpu.SemaphoreType.DMA((9,)),
            pltpu.SemaphoreType.DMA((chunks,)),
            pltpu.SemaphoreType.DMA((6,)),
            *[pltpu.SemaphoreType.DMA((copies,))] * 6,
        ],
        compiler_params=pltpu.CompilerParams(
            collective_id=0, has_side_effects=True, vmem_limit_bytes=127 * 512 * 1024
        ),
        cost_estimate=pl.CostEstimate(
            flops=2 * 8 * tokens * HQ * D, bytes_accessed=20 << 20, transcendentals=tokens * HQ
        ),
        name="decoder_layer",
    )(
        queries,
        memory,
        quarter_turns,
        token_order,
        lengths,
        attn_in,
        attn_out,
        attn_bias.transpose(1, 0, 2),
        ffn_in,
        ffn_in_bias,
        ffn_out,
        ffn_out_bias,
        norm_gain,
        norm_bias,
        query_pos,
        out_grad,
        jnp.asarray(position_table()),
    )
    outs = pl.pallas_call(
        finish_kernel,
        out_shape=[
            jax.ShapeDtypeStruct((1, NQ, D), bf16),
            jax.ShapeDtypeStruct((1, NQ, D), bf16),
            jax.ShapeDtypeStruct((1, tokens, D), bf16),
            jax.ShapeDtypeStruct((2, 3, D, D), f32),
            jax.ShapeDtypeStruct((2, D, D), f32),
            jax.ShapeDtypeStruct((3, 2, D), f32),
            jax.ShapeDtypeStruct((D, FF), f32),
            jax.ShapeDtypeStruct((1, FF), f32),
            jax.ShapeDtypeStruct((FF, D), f32),
            jax.ShapeDtypeStruct((1, D), f32),
            jax.ShapeDtypeStruct((3, D), f32),
            jax.ShapeDtypeStruct((3, D), f32),
            jax.ShapeDtypeStruct((NQ, D), f32),
        ],
        in_specs=[anywhere] * 6,
        out_specs=[anywhere] * 13,
        scratch_shapes=[
            pltpu.VMEM((tokens, D), bf16),
            *(pltpu.VMEM(shape, bf16) for shape in whole_shapes),
            pltpu.VMEM((NQ, D), bf16),
            pltpu.VMEM((NQ, D), bf16),
            pltpu.VMEM((2, 3, D, D), f32),
            pltpu.VMEM((2, D, D), f32),
            pltpu.VMEM((3, 2, D), f32),
            pltpu.VMEM((D, FF), f32),
            pltpu.VMEM((1, FF), f32),
            pltpu.VMEM((FF, D), f32),
            pltpu.VMEM((1, D), f32),
            pltpu.VMEM((3, D), f32),
            pltpu.VMEM((3, D), f32),
            pltpu.VMEM((NQ, D), f32),
            pltpu.SemaphoreType.DMA((8,)),
            pltpu.SemaphoreType.DMA((8,)),
            pltpu.SemaphoreType.DMA((5,)),
            pltpu.SemaphoreType.DMA((14,)),
        ],
        compiler_params=pltpu.CompilerParams(vmem_limit_bytes=62 * 1024 * 1024),
        name="write_outputs",
    )(*parts)
    return (
        *outs[:5],
        outs[5].transpose(1, 0, 2),
        outs[6],
        outs[7].reshape(FF),
        outs[8],
        outs[9].reshape(D),
        *outs[10:],
    )


def solution(mesh):
    in_specs = (
        P("dp", None, None),
        P("dp", "blk", None),
        P("dp"),
        P("dp", "blk"),
        P("dp"),
        P(),
        P(),
        P(),
        P(),
        P(),
        P(),
        P(),
        P(),
        P(),
        P(),
        P("dp", None, None),
    )
    out_specs = (
        P("dp", None, None),
        P("dp", None, None),
        P("dp", "blk", None),
        P(),
        P(),
        P(),
        P(),
        P(),
        P(),
        P(),
        P(),
        P(),
        P(),
    )
    layer = functools.partial(body, mesh.shape["dp"])
    return jax.shard_map(layer, mesh=mesh, in_specs=in_specs, out_specs=out_specs, check_vma=False)
```

profile of v0, /device:TPU:0, one launch (start us, length us, event | category | flops | bytes accessed | tf_op | source)
XLA Modules:
  0.0 93.8 jit_solution(8146220760175327348)
XLA Ops:
  1.9 85.4 %decoder_layer.1 = (bf16[125,256]{1,0:T(8,128)(2,1)}, bf16[125,256]{1,0:T(8,128)(2,1)}, bf16[1,8192,256]{2,1,0:T(8,128)(2,1)}, bf16[2,2048,256]{2,1,0:T(8,128)(2...) custom-call(bf16[1,125,256]{2,1,0:T(8,128)(2,1)} %queries_in.1, bf16[1,8192,256]{2,1,0:T(8,128)(2,1)} %memory_hbm.1, ...), custom_call_target="tpu_custom_call" | custom-call | flops 34359738368 | bytes 20971520 | tf_op jit(solution)/shard_map/decoder_layer/pallas_call | solution.py:1009
  87.3 6.5 %write_outputs.1 = (bf16[1,125,256]{2,1,0:T(8,128)(2,1)}, bf16[1,125,256]{2,1,0:T(8,128)(2,1)}, bf16[1,8192,256]{2,1,0:T(8,128)(2,1)}, f32[2,3,256,256]{3,2,1,0:...) custom-call(bf16[125,256]{1,0:T(8,128)(2,1)} %get-tuple-element.32.r, ...), custom_call_target="tpu_custom_call" | custom-call | tf_op jit(solution)/shard_map/write_outputs/pallas_call | solution.py:1095
where the time goes:
time: 94 us; the launch traced here: 93.8 us
  Pallas kernels  91.9 us (98%)
  between operations  1.95 us (2%)
    pallas_call x1, Pallas kernels, body(): pl.pallas_call(functools.partial(layer_kernel, tokens, pages), out_shape=...  85.4 us
    pallas_call x1, Pallas kernels, body(): pl.pallas_call(finish_kernel, out_shape=[jax.ShapeDtypeStruct((1, NQ, D),...  6.46 us

commit v1 on v0

--- a/solution.py
+++ b/solution.py
@@ -429,7 +429,11 @@
     for peer in peers:
         pl.semaphore_signal(barrier, inc=1, device_id=peer, device_id_type=pl.DeviceIdType.MESH)
 
-    load_memory = pltpu.make_async_copy(memory_hbm.at[0], memory_s, load_sem.at[0])
+    parts = [slice(0, 4 * CHUNK), slice(4 * CHUNK, tokens)]
+    load_memory = [
+        pltpu.make_async_copy(memory_hbm.at[0, part], memory_s.at[part], load_sem.at[k])
+        for part, k in zip(parts, (0, 9))
+    ]
     half = FF // 2
     ffn_in_s = [grad_scores_s.at[D * k : D * k + D] for k in range(2)]
     ffn_out_s = grad_scores_s.at[2 * D : 2 * D + FF, :D]
@@ -441,8 +445,7 @@
         for k in range(2)
     ]
     load_ffn.append(pltpu.make_async_copy(ffn_out_hbm, ffn_out_s, load_sem.at[3]))
-    load_memory.start()
-    for load in load_ffn:
+    for load in load_memory + load_ffn:
         load.start()
 
     pairs = [attn_bias[j].astype(f32) for j in range(3)]
@@ -482,17 +485,6 @@
     probs_self = raised / jnp.sum(raised, axis=0, keepdims=True)
     probs_self_b = probs_self.astype(bf16)
     value_t = value_self.astype(f32).T.astype(bf16)
-    attended = own_blocks(
-        [dot(value_t[pair_rows(p)], probs_self_b[:, pair_cols(p)]) for p in range(4)]
-    ).T.astype(bf16)
-    first_normed, first_rstd = norm_forward(queries_f + dot(attended, attn_out[0]) + bias[2:3])
-    first = first_normed * gain[0:1] + shift[0:1]
-    cross_q = (first + pos_f).astype(bf16)
-    query_c = (dot(cross_q, attn_in[1, 0]) + bias[3:4]).astype(bf16)
-    query_x = spread_rows(query_c.astype(f32))
-    query_k = dot(attn_in[1, 1], spread_cols(query_c.astype(f32).T))
-    query_kt[...] = (query_k * (scale * log2e)).astype(bf16)
-    back_s[:HQ] = (dot_nt(query_x, attn_in[1, 1]) * scale).astype(bf16)
     table = table_in[...]
     nothing = jnp.zeros((SIDE, D // 2), f32)
     table = jnp.concatenate(
@@ -502,7 +494,6 @@
     table_s[: 2 * SIDE] = table_high
     table_s[2 * SIDE :] = (table - table_high.astype(f32)).astype(bf16)
 
-    load_memory.wait()
     def mask_view(i):
         side, place = i // (chunks // 2), lax.rem(i, chunks // 2)
         return grad_scores_s.at[
@@ -512,8 +503,7 @@
 
     lane = lax.broadcasted_iota(jnp.int32, (CHUNK, NP), 1)
 
-    @pl.loop(0, chunks)
-    def _(i):
+    def place_chunk(i):
         rows = pl.ds(pl.multiple_of(i * CHUNK, CHUNK), CHUNK)
         line = code_s[:, rows]
         code = jnp.concatenate(
@@ -529,6 +519,24 @@
         masked = jnp.where(code < SIDE * SIDE, 0.0, masked_score)
         mask_view(i)[...] = masked.astype(bf16)
         key_in_s[rows] = (memory_s[rows].astype(f32) + dot(hot, table_s[...])).astype(bf16)
+
+    load_memory[0].wait()
+    attended = own_blocks(
+        [dot(value_t[pair_rows(p)], probs_self_b[:, pair_cols(p)]) for p in range(4)]
+    ).T.astype(bf16)
+    place_chunk(0)
+    first_normed, first_rstd = norm_forward(queries_f + dot(attended, attn_out[0]) + bias[2:3])
+    place_chunk(1)
+    first = first_normed * gain[0:1] + shift[0:1]
+    cross_q = (first + pos_f).astype(bf16)
+    query_c = (dot(cross_q, attn_in[1, 0]) + bias[3:4]).astype(bf16)
+    place_chunk(2)
+    query_k = dot(attn_in[1, 1], spread_cols(query_c.astype(f32).T))
+    query_kt[...] = (query_k * (scale * log2e)).astype(bf16)
+    place_chunk(3)
+    back_s[:HQ] = (dot_nt(spread_rows(query_c.astype(f32)), attn_in[1, 1]) * scale).astype(bf16)
+    load_memory[1].wait()
+    pl.loop(4, chunks)(place_chunk)
 
     def score_pair(p, key_in, mask, score_s):
         cols = pair_cols(p)
@@ -762,6 +770,7 @@
     grad_query_s = (
         own_blocks([dot(key_t[pair_rows(p)], grad_scores[:, pair_cols(p)]) for p in range(4)]) * scale
     ).T.astype(bf16)
+    take(queue_f)
     grad_key_s = (dot(grad_scores, spread_rows(query_self.astype(f32))) * scale).astype(bf16)
     grad_value_s = dot(probs_self_b, spread_rows(grad_attended)).astype(bf16)
     grad_mixed_q = dot_nt(grad_query_s, attn_in[0, 0]) + dot_nt(grad_key_s, attn_in[0, 1])
@@ -798,7 +807,6 @@
 
     take(queue_t)
     take(queue_k)
-    take(queue_f)
 
     @pl.loop(0, chunks)
     def _(i):
@@ -809,11 +817,11 @@
         at(
             i,
             [
+                (1, queue_f),
                 (3, queue_t),
                 (4, queue_k),
                 (7, queue_t),
                 (8, queue_k),
-                (9, queue_f),
                 (11, queue_t),
                 (12, queue_k),
                 (15, queue_t),
@@ -1061,7 +1069,7 @@
             pltpu.VMEM((D, NP), bf16),
             pltpu.VMEM((32, D), f32),
             *sum_buffers,
-            pltpu.SemaphoreType.DMA((9,)),
+            pltpu.SemaphoreType.DMA((10,)),
             pltpu.SemaphoreType.DMA((chunks,)),
             pltpu.SemaphoreType.DMA((6,)),
             *[pltpu.SemaphoreType.DMA((copies,))] * 6,

time: 94 us -> 95 us (1.011)
  no operation moved by 1% of the time
where the time goes in v1:
time: 95 us; the launch traced here: 94.9 us
  Pallas kernels  92.8 us (98%)
  between operations  2.11 us (2%)
    pallas_call x1, Pallas kernels, body(): pl.pallas_call(functools.partial(layer_kernel, tokens, pages), out_shape=...  86.3 us
    pallas_call x1, Pallas kernels, body(): pl.pallas_call(finish_kernel, out_shape=[jax.ShapeDtypeStruct((1, NQ, D),...  6.46 us

profile of v1, /device:TPU:0, one launch (start us, length us, event | category | flops | bytes accessed | tf_op | source)
XLA Modules:
  0.0 94.9 jit_solution(16419136424302052336)
XLA Ops:
  1.9 86.3 %decoder_layer.1 = (bf16[125,256]{1,0:T(8,128)(2,1)}, bf16[125,256]{1,0:T(8,128)(2,1)}, bf16[1,8192,256]{2,1,0:T(8,128)(2,1)}, bf16[2,2048,256]{2,1,0:T(8,128)(2...) custom-call(bf16[1,125,256]{2,1,0:T(8,128)(2,1)} %queries_in.1, bf16[1,8192,256]{2,1,0:T(8,128)(2,1)} %memory_hbm.1, ...), custom_call_target="tpu_custom_call" | custom-call | flops 34359738368 | bytes 20971520 | tf_op jit(solution)/shard_map/decoder_layer/pallas_call | solution.py:1017
  88.3 6.5 %write_outputs.1 = (bf16[1,125,256]{2,1,0:T(8,128)(2,1)}, bf16[1,125,256]{2,1,0:T(8,128)(2,1)}, bf16[1,8192,256]{2,1,0:T(8,128)(2,1)}, f32[2,3,256,256]{3,2,1,0:...) custom-call(bf16[125,256]{1,0:T(8,128)(2,1)} %get-tuple-element.32.r, ...), custom_call_target="tpu_custom_call" | custom-call | tf_op jit(solution)/shard_map/write_outputs/pallas_call | solution.py:1103

commit v2 on v0

--- a/solution.py
+++ b/solution.py
@@ -450,6 +450,12 @@
     gain = norm_gain[...].astype(f32)
     shift = norm_bias[...].astype(f32)
 
+    def each_two(block):
+        @pl.loop(0, chunks // 2)
+        def _(j):
+            block(j * 2)
+            block(j * 2 + 1)
+
     order = order_in[...]
     turn = turns_in[0]
     row_at = order >> 7
@@ -512,7 +518,7 @@
 
     lane = lax.broadcasted_iota(jnp.int32, (CHUNK, NP), 1)
 
-    @pl.loop(0, chunks)
+    @each_two
     def _(i):
         rows = pl.ds(pl.multiple_of(i * CHUNK, CHUNK), CHUNK)
         line = code_s[:, rows]
@@ -714,10 +720,9 @@
 
     def at(i, steps):
         for step, queue in steps:
-            pl.when(i == (step * chunks) // 16)(queue.pop(0))
-
-    @pl.loop(0, chunks)
-    def _(i):
+            pl.when(i == (step * chunks) // 32)(queue.pop(0))
+
+    def slope_block(i):
         rows = pl.ds(pl.multiple_of(i * CHUNK, CHUNK), CHUNK)
         key_ct = key_in_s[rows].T
         memory_c = memory_s[rows]
@@ -728,6 +733,11 @@
             probs_s[rows, cols] = probs.astype(bf16)
             grad_scores_s[rows, cols] = (probs * (grad_probs - inner[:, cols])).astype(bf16)
         mixed_s[...] += dot(key_ct, grad_scores_s[rows])
+
+    @pl.loop(0, chunks // 2)
+    def _(i):
+        slope_block(i * 2)
+        slope_block(i * 2 + 1)
         at(i, [(3, queue_f), (9, queue_f), (15, queue_f)])
 
     send_b[...] = (project_heads(key_wt, mixed_s[...]) * scale).astype(bf16)
@@ -800,12 +810,16 @@
     take(queue_k)
     take(queue_f)
 
-    @pl.loop(0, chunks)
-    def _(i):
+    def memory_block(i):
         rows = pl.ds(pl.multiple_of(i * CHUNK, CHUNK), CHUNK)
         both = jnp.concatenate([grad_scores_s[rows], probs_s[rows]], axis=1)
         memory_s[rows] = dot(both, back_s[...]).astype(bf16)
         pltpu.make_async_copy(memory_s.at[rows], memory_grad_hbm.at[0, rows], store_sem.at[i]).start()
+
+    @pl.loop(0, chunks // 2)
+    def _(i):
+        memory_block(i * 2)
+        memory_block(i * 2 + 1)
         at(
             i,
             [

time: 94 us -> 93 us (0.989)
  Pallas kernels: 91.9 us -> 90.7 us
    pallas_call x1, Pallas kernels: 85.4 us -> 84.2 us  [body(): pl.pallas_call(functools.partial(layer_kernel, tokens, pages), out_shape=...]
where the time goes in v2:
time: 93 us; the launch traced here: 92.8 us
  Pallas kernels  90.7 us (98%)
  between operations  2.11 us (2%)
    pallas_call x1, Pallas kernels, body(): pl.pallas_call(functools.partial(layer_kernel, tokens, pages), out_shape=...  84.2 us
    pallas_call x1, Pallas kernels, body(): pl.pallas_call(finish_kernel, out_shape=[jax.ShapeDtypeStruct((1, NQ, D),...  6.46 us

profile of v2, /device:TPU:0, one launch (start us, length us, event | category | flops | bytes accessed | tf_op | source)
XLA Modules:
  0.0 92.8 jit_solution(1597869429951849665)
XLA Ops:
  1.9 84.2 %decoder_layer.1 = (bf16[125,256]{1,0:T(8,128)(2,1)}, bf16[125,256]{1,0:T(8,128)(2,1)}, bf16[1,8192,256]{2,1,0:T(8,128)(2,1)}, bf16[2,2048,256]{2,1,0:T(8,128)(2...) custom-call(bf16[1,125,256]{2,1,0:T(8,128)(2,1)} %queries_in.1, bf16[1,8192,256]{2,1,0:T(8,128)(2,1)} %memory_hbm.1, ...), custom_call_target="tpu_custom_call" | custom-call | flops 34359738368 | bytes 20971520 | tf_op jit(solution)/shard_map/decoder_layer/pallas_call | solution.py:1023
  86.2 6.5 %write_outputs.1 = (bf16[1,125,256]{2,1,0:T(8,128)(2,1)}, bf16[1,125,256]{2,1,0:T(8,128)(2,1)}, bf16[1,8192,256]{2,1,0:T(8,128)(2,1)}, f32[2,3,256,256]{3,2,1,0:...) custom-call(bf16[125,256]{1,0:T(8,128)(2,1)} %get-tuple-element.32.r, ...), custom_call_target="tpu_custom_call" | custom-call | tf_op jit(solution)/shard_map/write_outputs/pallas_call | solution.py:1109

commit v3 on v2

--- a/solution.py
+++ b/solution.py
@@ -561,6 +561,9 @@
                 cols = pair_cols(p)
                 before = highest_s[0:1, cols]
                 highest = jnp.maximum(before, jnp.max(top_s[:, cols], axis=0, keepdims=True))
+                if p >= 2:
+                    earlier = jnp.minimum(top_s[0:1, pair_cols(p - 2)], -3.3e38)
+                    highest = jnp.maximum(highest, earlier)
                 highest_s[0:1, cols] = highest
                 shifts_s[pl.ds(i, 1), cols] = highest
                 fade = jnp.exp2(before - highest)

time: 93 us -> 93.4 us (level)
  no operation moved by 1% of the time
where the time goes in v3:
time: 93.4 us; the launch traced here: 93.2 us
  Pallas kernels  91.1 us (98%)
  between operations  2.11 us (2%)
    pallas_call x1, Pallas kernels, body(): pl.pallas_call(functools.partial(layer_kernel, tokens, pages), out_shape=...  84.7 us
    pallas_call x1, Pallas kernels, body(): pl.pallas_call(finish_kernel, out_shape=[jax.ShapeDtypeStruct((1, NQ, D),...  6.46 us

profile of v3, /device:TPU:0, one launch (start us, length us, event | category | flops | bytes accessed | tf_op | source)
XLA Modules:
  0.0 93.2 jit_solution(6567697142687645606)
XLA Ops:
  1.9 84.7 %decoder_layer.1 = (bf16[125,256]{1,0:T(8,128)(2,1)}, bf16[125,256]{1,0:T(8,128)(2,1)}, bf16[1,8192,256]{2,1,0:T(8,128)(2,1)}, bf16[2,2048,256]{2,1,0:T(8,128)(2...) custom-call(bf16[1,125,256]{2,1,0:T(8,128)(2,1)} %queries_in.1, bf16[1,8192,256]{2,1,0:T(8,128)(2,1)} %memory_hbm.1, ...), custom_call_target="tpu_custom_call" | custom-call | flops 34359738368 | bytes 20971520 | tf_op jit(solution)/shard_map/decoder_layer/pallas_call | solution.py:1026
  86.6 6.5 %write_outputs.1 = (bf16[1,125,256]{2,1,0:T(8,128)(2,1)}, bf16[1,125,256]{2,1,0:T(8,128)(2,1)}, bf16[1,8192,256]{2,1,0:T(8,128)(2,1)}, f32[2,3,256,256]{3,2,1,0:...) custom-call(bf16[125,256]{1,0:T(8,128)(2,1)} %get-tuple-element.32.r, ...), custom_call_target="tpu_custom_call" | custom-call | tf_op jit(solution)/shard_map/write_outputs/pallas_call | solution.py:1112

commit v4 on v2

--- a/solution.py
+++ b/solution.py
@@ -450,12 +450,6 @@
     gain = norm_gain[...].astype(f32)
     shift = norm_bias[...].astype(f32)
 
-    def each_two(block):
-        @pl.loop(0, chunks // 2)
-        def _(j):
-            block(j * 2)
-            block(j * 2 + 1)
-
     order = order_in[...]
     turn = turns_in[0]
     row_at = order >> 7
@@ -518,8 +512,7 @@
 
     lane = lax.broadcasted_iota(jnp.int32, (CHUNK, NP), 1)
 
-    @each_two
-    def _(i):
+    def place_block(i):
         rows = pl.ds(pl.multiple_of(i * CHUNK, CHUNK), CHUNK)
         line = code_s[:, rows]
         code = jnp.concatenate(
@@ -535,6 +528,11 @@
         masked = jnp.where(code < SIDE * SIDE, 0.0, masked_score)
         mask_view(i)[...] = masked.astype(bf16)
         key_in_s[rows] = (memory_s[rows].astype(f32) + dot(hot, table_s[...])).astype(bf16)
+
+    @pl.loop(0, chunks // 4)
+    def _(j):
+        for k in range(4):
+            place_block(j * 4 + k)
 
     def score_pair(p, key_in, mask, score_s):
         cols = pair_cols(p)

time: 93 us -> 92.4 us (level)
  no operation moved by 1% of the time
where the time goes in v4:
time: 92.4 us; the launch traced here: 92.3 us
  Pallas kernels  90.2 us (98%)
  between operations  2.11 us (2%)
    pallas_call x1, Pallas kernels, body(): pl.pallas_call(functools.partial(layer_kernel, tokens, pages), out_shape=...  83.7 us
    pallas_call x1, Pallas kernels, body(): pl.pallas_call(finish_kernel, out_shape=[jax.ShapeDtypeStruct((1, NQ, D),...  6.46 us

profile of v4, /device:TPU:0, one launch (start us, length us, event | category | flops | bytes accessed | tf_op | source)
XLA Modules:
  0.0 92.3 jit_solution(1959132240730216128)
XLA Ops:
  1.9 83.7 %decoder_layer.1 = (bf16[125,256]{1,0:T(8,128)(2,1)}, bf16[125,256]{1,0:T(8,128)(2,1)}, bf16[1,8192,256]{2,1,0:T(8,128)(2,1)}, bf16[2,2048,256]{2,1,0:T(8,128)(2...) custom-call(bf16[1,125,256]{2,1,0:T(8,128)(2,1)} %queries_in.1, bf16[1,8192,256]{2,1,0:T(8,128)(2,1)} %memory_hbm.1, ...), custom_call_target="tpu_custom_call" | custom-call | flops 34359738368 | bytes 20971520 | tf_op jit(solution)/shard_map/decoder_layer/pallas_call | solution.py:1021
  85.7 6.5 %write_outputs.1 = (bf16[1,125,256]{2,1,0:T(8,128)(2,1)}, bf16[1,125,256]{2,1,0:T(8,128)(2,1)}, bf16[1,8192,256]{2,1,0:T(8,128)(2,1)}, f32[2,3,256,256]{3,2,1,0:...) custom-call(bf16[125,256]{1,0:T(8,128)(2,1)} %get-tuple-element.32.r, ...), custom_call_target="tpu_custom_call" | custom-call | tf_op jit(solution)/shard_map/write_outputs/pallas_call | solution.py:1107

commit v5 on v4

--- a/solution.py
+++ b/solution.py
@@ -730,7 +730,7 @@
             probs = probs_s[rows, cols].astype(f32) * factor_s[pl.ds(i, 1), cols]
             probs_s[rows, cols] = probs.astype(bf16)
             grad_scores_s[rows, cols] = (probs * (grad_probs - inner[:, cols])).astype(bf16)
-        mixed_s[...] += dot(key_ct, grad_scores_s[rows])
+            mixed_s[:, cols] += dot(key_ct, grad_scores_s[rows, cols])
 
     @pl.loop(0, chunks // 2)
     def _(i):

time: 92.4 us -> 92.8 us (level)
  no operation moved by 1% of the time
where the time goes in v5:
time: 92.8 us; the launch traced here: 92.6 us
  Pallas kernels  90.5 us (98%)
  between operations  2.11 us (2%)
    pallas_call x1, Pallas kernels, body(): pl.pallas_call(functools.partial(layer_kernel, tokens, pages), out_shape=...  84 us
    pallas_call x1, Pallas kernels, body(): pl.pallas_call(finish_kernel, out_shape=[jax.ShapeDtypeStruct((1, NQ, D),...  6.46 us

profile of v5, /device:TPU:0, one launch (start us, length us, event | category | flops | bytes accessed | tf_op | source)
XLA Modules:
  0.0 92.6 jit_solution(6299402300511080915)
XLA Ops:
  1.9 84.0 %decoder_layer.1 = (bf16[125,256]{1,0:T(8,128)(2,1)}, bf16[125,256]{1,0:T(8,128)(2,1)}, bf16[1,8192,256]{2,1,0:T(8,128)(2,1)}, bf16[2,2048,256]{2,1,0:T(8,128)(2...) custom-call(bf16[1,125,256]{2,1,0:T(8,128)(2,1)} %queries_in.1, bf16[1,8192,256]{2,1,0:T(8,128)(2,1)} %memory_hbm.1, ...), custom_call_target="tpu_custom_call" | custom-call | flops 34359738368 | bytes 20971520 | tf_op jit(solution)/shard_map/decoder_layer/pallas_call | solution.py:1021
  86.0 6.5 %write_outputs.1 = (bf16[1,125,256]{2,1,0:T(8,128)(2,1)}, bf16[1,125,256]{2,1,0:T(8,128)(2,1)}, bf16[1,8192,256]{2,1,0:T(8,128)(2,1)}, f32[2,3,256,256]{3,2,1,0:...) custom-call(bf16[125,256]{1,0:T(8,128)(2,1)} %get-tuple-element.32.r, ...), custom_call_target="tpu_custom_call" | custom-call | tf_op jit(solution)/shard_map/write_outputs/pallas_call | solution.py:1107
